TPU v7x, 32 devices: a whole 2x2x4 slice. The times are simulated.
32 devices in a mesh: ang: 4 (over y, x), slab: 8 (over z, core).
Axes of the slice: x: 2, y: 2, z: 4, core: 2. Of those that a mesh axis runs over, the one named last changes fastest.
Arguments:
- projections: bfloat16 [16, 1024, 2048], P('slab', 'ang'), may hold values from -6 to 6
- dest_plane: int32 [16, 1024], P('slab'), may hold values from 0 to 255, as said below
- sub_offset: int32 [16, 1024], P('slab'), may hold values from 0 to 7, as said below
- ky_bin: int32 [16, 1024], P('slab'), may hold values from 0 to 7, as said below
Outputs:
- volume_real: float32 [256, 8, 2048], P('slab', None, 'ang')
- volume_imag: float32 [256, 8, 2048], P('slab', None, 'ang')
Inputs may be any that keep to these rules, and one draw needn't show every extreme that they name: With f = q for q < 512 and q - 1024 otherwise, and an integer s of 8 to 16 for each projection, e = floor(64 * 256 f / (1024 * s)) and dest_plane = floor(e / 8) + 128. Among the 2 projections of one slab index at most 512 rows fall on one aligned block of 32 planes; some slab index reaches 512. sub_offset = e mod 8 for the e of dest_plane. With f as for dest_plane and an integer r of 1 to 8 for each projection, ky_bin = floor((f + 512) r / 1024).
All inputs are finite; a program needn't handle non-finite values.
Results may differ from a plain program's by a relative error of at most 0.0085.
Values may be sent and summed in bfloat16 or wider, within the bound.
A program may use at most 192 MiB of HBM per device.

v0:
```python
import math

import jax
import jax.numpy as jnp
from jax import lax
from jax.sharding import PartitionSpec as P

Z_DEV = 32
KY = 8
REG_ITERS = 2


def padded(block, sides, width):
    for axis, dim in sides:
        count = lax.axis_size(axis)
        forward = [(i, i + 1) for i in range(count - 1)]
        backward = [(target, source) for source, target in forward]
        low = lax.ppermute(
            lax.slice_in_dim(block, block.shape[dim] - width, None, axis=dim), axis, forward
        )
        high = lax.ppermute(lax.slice_in_dim(block, 0, width, axis=dim), axis, backward)
        block = jnp.concatenate([low, block, high], axis=dim)
    return block


def trig_tables(length):
    row_index = jnp.arange(length, dtype=jnp.int32)[:, None]
    column = jnp.arange(length, dtype=jnp.int32)[None, :]
    phase_angle = (row_index * column % length).astype(jnp.float32) * (2.0 * math.pi / length)
    return (jnp.cos(phase_angle).astype(jnp.bfloat16), jnp.sin(phase_angle).astype(jnp.bfloat16))


def grid_rows(slots, centre, eighth, ky_index, rows, density):
    buffer = jnp.zeros((slots * KY, rows.shape[1]), jnp.float32)
    for shift in range(-2, 4):
        distance = shift - eighth.astype(jnp.float32) * 0.125
        weight = (jnp.exp(-0.5 * distance * distance) * density).astype(jnp.bfloat16)
        weight = lax.optimization_barrier(weight).astype(jnp.float32)
        index = (centre + (shift + 3)) * KY + ky_index
        buffer = buffer.at[index].add(weight[:, None] * rows)
    return buffer.reshape(slots, KY, rows.shape[1])


def on_device(projections, dest_plane, sub_offset, ky_bin):
    count_ang = lax.axis_size("ang")
    count_slab = lax.axis_size("slab")
    local_count, quarter, full_width = projections.shape
    height = quarter * count_ang
    cosines_w, sines_w = trig_tables(full_width)
    table = jnp.concatenate([cosines_w, sines_w], axis=1)
    transformed = jnp.dot(
        projections.reshape(local_count * quarter, full_width),
        table,
        preferred_element_type=jnp.float32,
    )
    row_spectra = jnp.stack([transformed[:, :full_width], -transformed[:, full_width:]], axis=1)
    row_spectra = row_spectra.astype(jnp.bfloat16).reshape(local_count, quarter, 2, full_width)
    cosines_h, sines_h = trig_tables(height)
    unitary = 1.0 / math.sqrt(height * full_width)
    exchanged = lax.all_to_all(row_spectra, "ang", split_axis=3, concat_axis=1, tiled=True)
    flattened = exchanged.reshape(exchanged.shape[0], height, -1)
    half_cols = exchanged.shape[3]
    cosine_part = jnp.einsum(
        "qh,phx->pqx", cosines_h, flattened, preferred_element_type=jnp.float32
    )
    sine_part = jnp.einsum("qh,phx->pqx", sines_h, flattened, preferred_element_type=jnp.float32)
    real_part = cosine_part[:, :, :half_cols] + sine_part[:, :, half_cols:]
    imag_part = cosine_part[:, :, half_cols:] - sine_part[:, :, :half_cols]
    spectrum = (jnp.concatenate([real_part, imag_part], axis=2) * unitary).astype(jnp.bfloat16)
    spectral_rows = spectrum.reshape(local_count * height, -1)
    total_cols = spectral_rows.shape[1]
    planes_all = dest_plane.reshape(-1)
    eighths_all = sub_offset.reshape(-1)
    ky_all = ky_bin.reshape(-1)
    density = 1.0 / math.sqrt(local_count * count_slab)
    whole = grid_rows(
        Z_DEV * count_slab + 6, planes_all, eighths_all, ky_all, spectral_rows, density
    )
    gridded = lax.psum_scatter(
        whole[3:-3].astype(jnp.bfloat16), "slab", scatter_dimension=0, tiled=True
    ).astype(jnp.float32)
    iterate = gridded
    for sweep in range(REG_ITERS):
        bordered_planes = padded(iterate.astype(jnp.bfloat16), (("slab", 0),), 1).astype(
            iterate.dtype
        )
        iterate = iterate - 0.25 * (
            iterate - gridded + (2.0 * iterate - bordered_planes[:-2] - bordered_planes[2:])
        )
    half_cols = total_cols // 2
    return (iterate[:, :, :half_cols], iterate[:, :, half_cols:])


def solution(mesh):
    placed = (P("slab", "ang", None), P("slab", None), P("slab", None), P("slab", None))
    return jax.shard_map(
        on_device,
        mesh=mesh,
        in_specs=placed,
        out_specs=(P("slab", None, "ang"), P("slab", None, "ang")),
        check_vma=False,
    )
```

profile of v0, /device:TPU:17, one launch (start us, length us, event | category | flops | bytes accessed | tf_op | source)
XLA Modules:
  0.0 490.4 jit_solution(2676022399908207777)
XLA Ops:
  7.2 0.0 copy-start
  7.2 67.8 %sine_convert_fusion = (bf16[2048,2048]{1,0:T(8,128)(2,1)}, bf16[2048,2048]{1,0:T(8,128)(2,1)}) fusion(), kind=kLoop, calls=%fused_computation.22 | loop fusion | flops 67108864 | bytes 16777216 | tf_op jit(solution)/shard_map/convert_element_type | solution.py:30
  75.0 0.0 copy-done
  75.0 17.8 %fusion.17 = f32[512,4096]{1,0:T(8,128)} fusion(bf16[512,2048]{1,0:T(8,128)(2,1)S(1)} %bitcast.84, bf16[2048,2048]{1,0:T(8,128)(2,1)} %get-tuple-element.22, bf16[2048,2048]{1,0:T(8,128)(2,1)} %get-tuple-element.23), kind=kOutput, calls=%fused_computation.36 | convolution fusion | flops 8623489024 | bytes 27262976 | tf_op jit(solution)/shard_map/dot_general | solution.py:51
  92.8 2.7 fusion.25
  95.5 3.9 slice.115
  99.3 6.1 %copy.7 = bf16[2,256,1,2048]{1,0,2,3:T(2,128)(2,1)} copy(bf16[2,256,1,2048]{3,1,0,2:T(8,128)(2,1)} %bitcast.99) | data formatting | bytes 4194304 | tf_op jit(solution)/shard_map/stack | solution.py:56
  105.5 3.9 copy.8
  109.4 0.0 copy-start.3
  109.4 0.0 copy-start.4
  109.4 0.0 copy-start.5
  109.4 9.1 %pad_maximum_fusion = bf16[2,256,2,2048]{1,0,2,3:T(2,128)(2,1)} fusion(bf16[2,256,1,2048]{1,0,2,3:T(2,128)(2,1)} %copy.8, bf16[2,256,1,2048]{1,0,2,3:T(2,128)(2,1)} %copy.7), kind=kLoop, calls=%fused_computation.50 | loop fusion | flops 2097152 | bytes 8388608 | tf_op jit(solution)/shard_map/stack | solution.py:56
  118.4 4.8 all-to-all-start
  123.3 0.6 reduce-scatter.2.cloned.1.call-start
  123.9 0.0 copy-done.3
  123.9 0.0 copy-done.4
  123.9 0.0 copy-done.5
  124.3 45.9 %all-to-all-done = bf16[2,256,2,2048]{1,0,2,3:T(2,128)(2,1)} async-done(((bf16[2,256,2,2048]{1,0,2,3:T(2,128)(2,1)}), bf16[2,256,2,2048]{1,0,2,3:T(2,128)(2,1)}, u32[]{:S(2)}, u32[]{:S(2)}) %all-to-all-start) | async-done | bytes 4194336 | tf_op jit(solution)/shard_map/all_to_all | solution.py:60
  170.2 20.1 %copy.9 = bf16[2,256,2,4,512]{4,2,1,3,0:T(2,128)(2,1)} copy(bf16[2,256,2,4,512]{1,0,2,4,3:T(2,128)(2,1)} %bitcast.5) | data formatting | bytes 8388608 | tf_op jit(solution)/shard_map/all_to_all | solution.py:60
  190.3 7.8 %reshape.271 = bf16[2,1024,1024]{2,1,0:T(8,128)(2,1)} reshape(bf16[2,4,256,2,512]{4,3,2,1,0:T(2,128)(2,1)} %bitcast.97) | data formatting | bytes 8388608 | tf_op jit(solution)/shard_map/reshape | solution.py:61
  198.1 23.4 %convolution_bitcast_fusion.1 = f32[2,1024,1024]{2,1,0:T(8,128)} fusion(bf16[2,1024,1024]{2,1,0:T(8,128)(2,1)} %reshape.271), kind=kOutput, calls=%fused_computation.63 | convolution fusion | flops 4310695936 | bytes 12582912 | tf_op jit(solution)/shard_map/qh,phx->pqx/dot_general | solution.py:63
  221.4 0.0 copy-done.2
  221.4 21.2 %convolution_bitcast_fusion = f32[2,1024,1024]{2,1,0:T(8,128)} fusion(bf16[2,1024,1024]{2,1,0:T(8,128)(2,1)S(1)} %copy-done.2), kind=kOutput, calls=%fused_computation.62 | convolution fusion | flops 4310695936 | bytes 12582912 | tf_op jit(solution)/shard_map/qh,phx->pqx/dot_general | solution.py:66
  242.6 11.2 %slice_add_fusion = (f32[2,1024,512]{2,1,0:T(8,128)}, f32[2,1024,512]{2,1,0:T(8,128)}) fusion(f32[2,1024,1024]{2,1,0:T(8,128)} %convolution_bitcast_fusion, f32[2,1024,1024]{2,1,0:T(8,128)} %convolution_bitcast_fusion.1), kind=kLoop, calls=%fused_computation.46 | loop fusion | flops 2097152 | bytes 25165824 | tf_op jit(solution)/shard_map/add | solution.py:67
  253.8 23.0 %scatter_custom_fusion = f32[2096,1024]{1,0:T(8,128)} fusion(s32[2048]{0:T(1024)S(1)} %bitcast.111, f32[]{:T(128)} %constant.25.clone.1, f32[2048]{0:T(1024)S(1)} %convert_element_type.100, f32[2048,512]{1,0:T(8,128)} %bitcast.91, f32[2048,512]{1,0:T(8,128)} %bitcast.85), kind=kCustom, calls=%fused_computation.27 | custom fusion | flops 12582912 | bytes 16982020 | tf_op jit(solution)/shard_map/scatter-add | solution.py:40
  276.8 26.1 %scatter_custom_fusion.1 = f32[2096,1024]{1,0:T(8,128)} fusion(f32[2096,1024]{1,0:T(8,128)} %scatter_custom_fusion, s32[2048]{0:T(1024)S(1)} %bitcast.110, f32[2048]{0:T(1024)S(1)} %convert_element_type.110, f32[2048,512]{1,0:T(8,128)} %bitcast.92, f32[2048,512]{1,0:T(8,128)} %bitcast.86), kind=kCustom, calls=%fused_computation.28 | custom fusion | flops 12582912 | bytes 16982016 | tf_op jit(solution)/shard_map/scatter-add | solution.py:40
  302.9 25.9 %scatter_custom_fusion.2 = f32[2096,1024]{1,0:T(8,128)} fusion(f32[2096,1024]{1,0:T(8,128)} %scatter_custom_fusion.1, s32[2048]{0:T(1024)S(1)} %bitcast.109, f32[2048]{0:T(1024)S(1)} %convert_element_type.112, f32[2048,512]{1,0:T(8,128)} %bitcast.93, f32[2048,512]{1,0:T(8,128)} %bitcast.87), kind=kCustom, calls=%fused_computation.29 | custom fusion | flops 12582912 | bytes 16982016 | tf_op jit(solution)/shard_map/scatter-add | solution.py:40
  328.8 26.1 %scatter_custom_fusion.3 = f32[2096,1024]{1,0:T(8,128)} fusion(f32[2096,1024]{1,0:T(8,128)} %scatter_custom_fusion.2, s32[2048]{0:T(1024)S(1)} %bitcast.107, f32[2048]{0:T(1024)S(1)} %convert_element_type.114, f32[2048,512]{1,0:T(8,128)} %bitcast.94, f32[2048,512]{1,0:T(8,128)} %bitcast.88), kind=kCustom, calls=%fused_computation.30 | custom fusion | flops 12582912 | bytes 16982016 | tf_op jit(solution)/shard_map/scatter-add | solution.py:40
  354.9 25.9 %scatter_custom_fusion.4 = f32[2096,1024]{1,0:T(8,128)} fusion(f32[2096,1024]{1,0:T(8,128)} %scatter_custom_fusion.3, s32[2048]{0:T(1024)S(1)} %bitcast.108, f32[2048]{0:T(1024)S(1)} %convert_element_type.116, f32[2048,512]{1,0:T(8,128)} %bitcast.95, f32[2048,512]{1,0:T(8,128)} %bitcast.89), kind=kCustom, calls=%fused_computation.31 | custom fusion | flops 12582912 | bytes 16982016 | tf_op jit(solution)/shard_map/scatter-add | solution.py:40
  380.7 26.1 %scatter_custom_fusion.5 = f32[2096,1024]{1,0:T(8,128)} fusion(f32[2096,1024]{1,0:T(8,128)} %scatter_custom_fusion.4, s32[2048]{0:T(1024)S(1)} %bitcast.106, f32[2048]{0:T(1024)S(1)} %convert_element_type.118, f32[2048,512]{1,0:T(8,128)} %bitcast.96, f32[2048,512]{1,0:T(8,128)} %bitcast.90), kind=kCustom, calls=%fused_computation.32 | custom fusion | flops 12582912 | bytes 16982016 | tf_op jit(solution)/shard_map/scatter-add | solution.py:40
  406.9 6.0 %fusion.24 = bf16[256,8,1024]{2,1,0:T(8,128)(2,1)} fusion(f32[2096,1024]{1,0:T(8,128)} %scatter_custom_fusion.5), kind=kLoop, calls=%fused_computation.44 | loop fusion | bytes 8388608 | tf_op jit(solution)/shard_map/convert_element_type | solution.py:80
  412.9 0.0 reduce-scatter.2.cloned.1.call-update
  412.9 49.4 %reduce-scatter.2.cloned.1.call-done = bf16[32,8,1024]{2,1,0:T(8,128)(2,1)} async-done(((bf16[256,8,1024]{2,1,0:T(8,128)(2,1)}), bf16[32,8,1024]{2,1,0:T(8,128)(2,1)}) %reduce-scatter.2.cloned.1.call-update) | async-done | bytes 524304 | tf_op jit(solution)/shard_map/reduce_scatter | solution.py:79
  462.4 0.7 fusion.78
  463.1 2.7 collective-permute-start
  465.8 1.9 collective-permute-start.1
  467.8 0.0 collective-permute-done
  467.8 3.1 collective-permute-done.1
  470.9 1.1 maximum_convert_fusion
  472.0 1.3 fusion.75
  473.4 1.9 collective-permute-start.2
  475.3 2.4 collective-permute-start.3
  477.7 0.0 collective-permute-done.2
  477.7 2.6 collective-permute-done.3
  480.4 0.1 maximum_convert_fusion.1
  480.5 1.6 fusion.47
  482.1 1.0 fusion.76
  483.1 0.0 copy-done.1
  (26 shorter events, 0.2 us)
Async XLA Ops:
  7.2 67.8 %copy-start = (bf16[2,256,2048]{2,1,0:T(8,128)(2,1)S(1)}, bf16[2,256,2048]{2,1,0:T(8,128)(2,1)}, u32[]{:S(2)}) copy-start(bf16[2,256,2048]{2,1,0:T(8,128)(2,1)} %param.4) | copy-start | bytes 6291460
  109.4 14.5 %copy-start.3 = (s32[2,1024]{1,0:T(2,128)S(1)}, s32[2,1024]{1,0:T(2,128)}, u32[]{:S(2)}) copy-start(s32[2,1024]{1,0:T(2,128)} %param.6) | copy-start | bytes 24580
  109.4 14.5 %copy-start.4 = (s32[2,1024]{1,0:T(2,128)S(1)}, s32[2,1024]{1,0:T(2,128)}, u32[]{:S(2)}) copy-start(s32[2,1024]{1,0:T(2,128)} %param.7) | copy-start | bytes 24580
  109.4 14.6 %copy-start.5 = (s32[2,1024]{1,0:T(2,128)S(1)}, s32[2,1024]{1,0:T(2,128)}, u32[]{:S(2)}) copy-start(s32[2,1024]{1,0:T(2,128)} %param.5) | copy-start | bytes 24580
  118.4 51.8 %all-to-all-start = ((bf16[2,256,2,2048]{1,0,2,3:T(2,128)(2,1)}), bf16[2,256,2,2048]{1,0,2,3:T(2,128)(2,1)}, u32[]{:S(2)}, u32[]{:S(2)}) async-start(bf16[2,256,2,2048]{1,0,2,3:T(2,128)(2,1)} %pad_maximum_fusion), calls=%async_computation | async-start | bytes 8388608 | tf_op jit(solution)/shard_map/all_to_all | solution.py:60
  123.3 339.1 %reduce-scatter.2.cloned.1.call-start = ((), (), s32[]{:S(2)}) async-start(), calls=%async_computation.2 | async-start | bytes 4718592 | tf_op jit(solution)/shard_map/reduce_scatter | solution.py:79
  198.1 23.4 %copy-start.2 = (bf16[2,1024,1024]{2,1,0:T(8,128)(2,1)S(1)}, bf16[2,1024,1024]{2,1,0:T(8,128)(2,1)}, u32[]{:S(2)}) copy-start(bf16[2,1024,1024]{2,1,0:T(8,128)(2,1)} %reshape.271) | copy-start | bytes 12582916
  412.9 70.2 %copy-start.1 = (bf16[2,256,2048]{2,1,0:T(8,128)(2,1)S(1)}, bf16[2,256,2048]{2,1,0:T(8,128)(2,1)}, u32[]{:S(2)}) copy-start(bf16[2,256,2048]{2,1,0:T(8,128)(2,1)} %param.4) | copy-start | bytes 6291460
  463.1 4.7 collective-permute-start
  465.8 5.1 %collective-permute-start.1 = (bf16[1,8,1024]{2,1,0:T(8,128)(2,1)S(1)}, bf16[1,8,1024]{2,1,0:T(8,128)(2,1)S(1)}, u32[]{:S(2)}, u32[]{:S(2)}) collective-permute-start(bf16[1,8,1024]{2,1,0:T(8,128)(2,1)S(1)} %get-tuple-element.9), channel_id=1, source_target_pairs={{1,0},{2,1},{3,2},{4,3},{5,4},{6,5},{7,6},{9,8},{10,9},{11,10},{12... | collective-permute-start | bytes 49160 | tf_op jit(solution)/shard_map/ppermute | solution.py:21
  473.4 4.3 collective-permute-start.2
  475.3 5.1 %collective-permute-start.3 = (bf16[1,8,1024]{2,1,0:T(8,128)(2,1)S(1)}, bf16[1,8,1024]{2,1,0:T(8,128)(2,1)S(1)}, u32[]{:S(2)}, u32[]{:S(2)}) collective-permute-start(bf16[1,8,1024]{2,1,0:T(8,128)(2,1)S(1)} %get-tuple-element.7), channel_id=1, source_target_pairs={{1,0},{2,1},{3,2},{4,3},{5,4},{6,5},{7,6},{9,8},{10,9},{11,10},{12... | collective-permute-start | bytes 49160 | tf_op jit(solution)/shard_map/ppermute | solution.py:21
Sparse Core Ops, SparseCore 0:
  413.1 49.2 reduce-scatter.1
where the time goes:
time: 500 us; the launch traced here: 490 us
  other arithmetic  248 us (50%)
  waiting for transfers between devices  101 us (20%)
  matrix products  62.4 us (12%)
  local copies, waits for them, and re-layouts  49.7 us (10%)
  between operations  14.8 us (3%)
  starting transfers between devices  14.4 us (3%)
    scatter-add x6, other arithmetic, grid_rows(): buffer = buffer.at[index].add(weight[:, None] * rows)  153 us
    convert_element_type x1, other arithmetic, trig_tables(): jnp.sin(phase_angle).astype(jnp.bfloat16)  67.8 us
    reduce_scatter x1, waiting for transfers between devices, on_device(): lax.psum_scatter(whole[3:-3].astype(jnp.bfloat16), 'slab', scatter_dimens...  49.4 us
    all_to_all x1, waiting for transfers between devices, on_device(): lax.all_to_all(row_spectra, 'ang', split_axis=3, concat_axis=1, tiled=True)  45.9 us
    dot_general x1, matrix products, on_device(): jnp.einsum('qh,phx->pqx', cosines_h, flattened, preferred_element_type=jn...  23.4 us
    dot_general x1, matrix products, on_device(): jnp.einsum('qh,phx->pqx', sines_h, flattened, preferred_element_type=jnp....  21.2 us
    all_to_all x1, local copies, waits for them, and re-layouts, on_device(): lax.all_to_all(row_spectra, 'ang', split_axis=3, concat_axis=1, tiled=True)  20.1 us
    dot_general x1, matrix products, on_device(): jnp.dot(projections.reshape(local_count * quarter, full_width), table, pr...  17.8 us
  transfers between devices with their start and end apart: 6, of which 4 were waited for; matrix products, arithmetic and copies ran while one was open for 0% of the time, Pallas kernels for 0%

commit v1 on v0

v1 whole, which is shorter than its diff:
```python
import functools
import math

import jax
import jax.numpy as jnp
import ml_dtypes
import numpy as np
from jax import lax
from jax.experimental import pallas as pl
from jax.experimental.pallas import tpu as pltpu
from jax.sharding import PartitionSpec as P

Z_DEV = 32
KY = 8
REG_ITERS = 2
SLOPE_LOW, SLOPE_HIGH = 8, 16
CHUNK = 256
BF16 = jnp.bfloat16
F32 = jnp.float32


def trig_values(length):
    phase = np.arange(length, dtype=np.float32) * np.float32(2.0 * math.pi / length)
    return np.cos(phase), np.sin(phase)


def column_table(width, groups):
    cos, sin = trig_values(width)
    count = width // 2 // groups
    w = np.arange(width)[:, None]
    tables = []
    for j in range(groups):
        phase = w * (groups * np.arange(count) + j)[None, :] % width
        real, imag = cos[phase], -sin[phase]
        if j == 0:
            imag[:, 0] = cos[w[:, 0] * (width // 2) % width]
        tables.append(np.concatenate([real, imag], axis=1))
    return np.stack(tables).astype(ml_dtypes.bfloat16)


def row_tables(height):
    cos, sin = trig_values(height)
    phase = np.arange(height // 2)[:, None] * np.arange(height)[None, :] % height
    cosines, sines = cos[phase], sin[phase]
    sines[0] = cos[np.arange(height) * (height // 2) % height]
    return cosines.astype(ml_dtypes.bfloat16), sines.astype(ml_dtypes.bfloat16)


def update_matrix(planes):
    eye = np.eye(planes)
    lap = 2.0 * eye - np.eye(planes, k=1) - np.eye(planes, k=-1)
    total = eye
    for sweep in range(REG_ITERS):
        total = total - 0.25 * ((total - eye) + lap @ total)
    return total.astype(ml_dtypes.bfloat16)


def placement(width, groups):
    block = width // groups
    half = block // groups
    out = np.zeros((groups, 2, groups * half, block), np.float32)
    for dest in range(groups):
        for j in range(groups):
            for m in range(half):
                if dest < groups // 2:
                    column, sign = groups * m + j, 1.0
                else:
                    column = block - (groups * m + j)
                    column, sign = (0 if j == 0 and m == 0 else column), -1.0
                out[dest, 0, j * half + m, column] = 1.0
                out[dest, 1, j * half + m, column] = sign
    return out.astype(ml_dtypes.bfloat16)


def needs(planes, height, local_count):
    half = height // 2
    per_sign = half // CHUNK
    table = np.zeros((planes // Z_DEV, 2, local_count * 2 * per_sign), np.int32)
    up = np.arange(half)
    down = np.concatenate([[-half], -np.arange(1, half)])
    mirror_up = np.concatenate([[0], -np.arange(1, half)])
    mirror_down = np.concatenate([[-half], np.arange(1, half)])
    for kind, signs in enumerate(((up, down), (mirror_up, mirror_down))):
        for sign, rows in enumerate(signs):
            for part in range(per_sign):
                f = rows[part * CHUNK : (part + 1) * CHUNK].astype(np.int64)
                reach = [(64 * planes * f // (height * s)) // 8 + planes // 2 for s in range(SLOPE_LOW, SLOPE_HIGH + 1)]
                low = np.min(reach, axis=0) - 2 - REG_ITERS
                high = np.max(reach, axis=0) + 3 + REG_ITERS
                for b in range(planes // Z_DEV):
                    hit = np.any((high >= b * Z_DEV) & (low < (b + 1) * Z_DEV))
                    for p in range(local_count):
                        table[b, kind, (p * 2 + sign) * per_sign + part] = int(hit)
    return table.reshape(-1)


def columns_kernel(x_ref, t_ref, o_ref):
    o_ref[0] = jnp.dot(x_ref[...], t_ref[0], preferred_element_type=F32).astype(o_ref.dtype)


def column_spectra(rows, table):
    groups, width, columns = table.shape
    count = rows.shape[0]
    return pl.pallas_call(
        columns_kernel,
        grid=(groups,),
        out_shape=jax.ShapeDtypeStruct((groups, count, columns), BF16),
        in_specs=[
            pl.BlockSpec((count, width), lambda j: (0, 0)),
            pl.BlockSpec((1, width, columns), lambda j: (j, 0, 0)),
        ],
        out_specs=pl.BlockSpec((1, count, columns), lambda j: (j, 0, 0)),
        compiler_params=pltpu.CompilerParams(vmem_limit_bytes=40 * 2**20),
        cost_estimate=pl.CostEstimate(
            flops=2 * count * width * columns * groups, bytes_accessed=12 * 2**20, transcendentals=0
        ),
    )(rows, table)


def grid_kernel(local_count, unitary, need_ref, r_ref, cos_ref, sin_ref, v_ref, ky_ref, o_ref, spec_d, spec_m, acc_d, acc_m):
    step = pl.program_id(0)
    half, height = cos_ref.shape
    columns = r_ref.shape[-1]
    quarter = columns // 4
    chunks = local_count * height // CHUNK

    @pl.when(step < local_count)
    def _():
        rows = r_ref[...].reshape(height, columns)
        cosine = jnp.dot(cos_ref[...], rows, preferred_element_type=F32)
        sine = jnp.dot(sin_ref[...], rows, preferred_element_type=F32)
        first = lax.broadcasted_iota(jnp.int32, (half, columns), 0) == 0
        other = jnp.where(first, sine, cosine)
        sine = jnp.where(first, 0.0, sine)
        lane = lax.broadcasted_iota(jnp.int32, (half, quarter), 1)
        packed = jnp.logical_and(lane == 0, lax.axis_index("ang") == 0)

        def part(a, i):
            return a[:, i * quarter : (i + 1) * quarter]

        for sign, (c, s) in enumerate(((cosine, sine), (other, -sine))):
            re0 = part(c, 0) + jnp.where(packed, 0.0, part(s, 2))
            im0 = jnp.where(packed, 0.0, part(c, 2)) - part(s, 0)
            re1 = part(c, 1) + part(s, 3)
            im1 = part(c, 3) - part(s, 1)
            re0m = jnp.where(packed, jnp.broadcast_to(re1[:, :1], re0.shape), re0)
            im0m = jnp.where(packed, jnp.broadcast_to(im1[:, :1], im0.shape), im0)
            re1m = jnp.where(packed, part(c, 2), re1)
            im1m = jnp.where(packed, -part(s, 2), im1)
            base = pl.multiple_of((step * 2 + sign) * half, half)
            for i, value in enumerate((re0, im0, re1, im1)):
                spec_d[pl.ds(base, half), i * quarter : (i + 1) * quarter] = (value * unitary).astype(BF16)
            for i, value in enumerate((re1m, im1m, re0m, im0m)):
                spec_m[pl.ds(base, half), i * quarter : (i + 1) * quarter] = (value * unitary).astype(BF16)

    @pl.when(step >= local_count)
    def _():
        block = step - local_count
        acc_d[...] = jnp.zeros_like(acc_d)
        acc_m[...] = jnp.zeros_like(acc_m)
        ky_row = lax.broadcasted_iota(jnp.int32, (KY, CHUNK), 0)
        for kind, (spec, acc) in enumerate(((spec_d, acc_d), (spec_m, acc_m))):
            for c in range(chunks):

                @pl.when(need_ref[(block * 2 + kind) * chunks + c] != 0)
                def _(kind=kind, spec=spec, acc=acc, c=c):
                    at = kind * chunks * CHUNK + c * CHUNK
                    weight = v_ref[:, at : at + CHUNK].astype(F32)
                    hit = ky_ref[:, at : at + CHUNK] == ky_row
                    spread = jnp.where(hit[None], weight[:, None, :], 0.0)
                    spread = spread.reshape(Z_DEV * KY, CHUNK).astype(BF16)
                    acc[...] += jnp.dot(spread, spec[c * CHUNK : (c + 1) * CHUNK, :], preferred_element_type=F32)

        for i, acc in enumerate((acc_d, acc_m)):
            for h in range(2):
                o_ref[0, i * 2 + h] = acc[:, h * 2 * quarter : (h + 1) * 2 * quarter].astype(BF16)


def gridded_blocks(received, weights, ky, planes, unitary):
    groups, local_count, quarter_rows, columns = received.shape
    height = groups * quarter_rows
    cosines, sines = row_tables(height)
    blocks = planes // Z_DEV
    chunk_count = local_count * height
    block_of = lambda i, need: (jnp.maximum(i - local_count, 0), 0)
    whole = lambda i, need: (0, 0)
    return pl.pallas_call(
        functools.partial(grid_kernel, local_count, unitary),
        out_shape=jax.ShapeDtypeStruct((blocks, 4, Z_DEV * KY, columns // 2), BF16),
        grid_spec=pltpu.PrefetchScalarGridSpec(
            num_scalar_prefetch=1,
            grid=(local_count + blocks,),
            in_specs=[
                pl.BlockSpec(
                    (groups, 1, quarter_rows, columns),
                    lambda i, need: (0, jnp.minimum(i, local_count - 1), 0, 0),
                ),
                pl.BlockSpec(cosines.shape, whole),
                pl.BlockSpec(sines.shape, whole),
                pl.BlockSpec((Z_DEV, 2 * chunk_count), block_of),
                pl.BlockSpec((1, 2 * chunk_count), whole),
            ],
            out_specs=pl.BlockSpec(
                (1, 4, Z_DEV * KY, columns // 2),
                lambda i, need: (jnp.maximum(i - local_count, 0), 0, 0, 0),
            ),
            scratch_shapes=[
                pltpu.VMEM((chunk_count, columns), BF16),
                pltpu.VMEM((chunk_count, columns), BF16),
                pltpu.VMEM((Z_DEV * KY, columns), F32),
                pltpu.VMEM((Z_DEV * KY, columns), F32),
            ],
        ),
        compiler_params=pltpu.CompilerParams(vmem_limit_bytes=48 * 2**20),
        cost_estimate=pl.CostEstimate(
            flops=2 * chunk_count * height * columns + 2 * blocks * Z_DEV * KY * chunk_count * columns,
            bytes_accessed=12 * 2**20,
            transcendentals=0,
        ),
    )(jnp.asarray(needs(planes, height, local_count)), received, jnp.asarray(cosines), jnp.asarray(sines), weights, ky)


def place_kernel(x_ref, p_ref, real_ref, imag_ref):
    groups, rows, columns = x_ref.shape
    half = columns // 2
    for i, out in enumerate((real_ref, imag_ref)):
        total = None
        for j in range(groups):
            term = jnp.dot(
                x_ref[j, :, i * half : (i + 1) * half],
                p_ref[0, i, j * half : (j + 1) * half, :],
                preferred_element_type=F32,
            )
            total = term if total is None else total + term
        out[...] = total


def placed_columns(received, table, me):
    groups, rows, columns = received.shape
    block = table.shape[-1]
    return pl.pallas_call(
        place_kernel,
        out_shape=[jax.ShapeDtypeStruct((rows, block), F32)] * 2,
        compiler_params=pltpu.CompilerParams(vmem_limit_bytes=40 * 2**20),
    )(received, lax.dynamic_slice_in_dim(table, me, 1, 0))


def slot_orders(values):
    half = values.shape[1] // 2
    low, high = values[:, :half], values[:, half:]
    back_high = high[:, :0:-1]
    direct = jnp.concatenate([low, high[:, :1], back_high], axis=1)
    mirror = jnp.concatenate([low[:, :1], back_high, high[:, :1], low[:, 1:]], axis=1)
    return jnp.concatenate([direct.reshape(1, -1), mirror.reshape(1, -1)], axis=1)


def plane_weights(dest, eighths, planes, density):
    plane = jnp.arange(planes, dtype=jnp.int32)[:, None]
    shift = plane - dest
    spread = jnp.zeros(shift.shape, BF16)
    for g in range(-2, 4):
        distance = g - eighths.astype(F32) * 0.125
        weight = (jnp.exp(-0.5 * distance * distance) * density).astype(BF16)
        spread = jnp.where(shift == g, weight, spread)
    update = jnp.asarray(update_matrix(planes))
    return jnp.dot(update, spread, preferred_element_type=F32).astype(BF16)


def on_device(projections, dest_plane, sub_offset, ky_bin):
    count_ang = lax.axis_size("ang")
    count_slab = lax.axis_size("slab")
    local_count, quarter, full_width = projections.shape
    height = quarter * count_ang
    planes = Z_DEV * count_slab
    unitary = 1.0 / math.sqrt(height * full_width)
    density = 1.0 / math.sqrt(local_count * count_slab)
    table = jnp.asarray(column_table(full_width, count_ang))
    spectra = column_spectra(projections.reshape(local_count * quarter, full_width), table)
    received = lax.all_to_all(spectra, "ang", split_axis=0, concat_axis=0, tiled=True)
    received = received.reshape(count_ang, local_count, quarter, -1)
    weights = plane_weights(slot_orders(dest_plane), slot_orders(sub_offset), planes, density)
    blocks = gridded_blocks(received, weights, slot_orders(ky_bin), planes, unitary)
    mine = lax.psum_scatter(blocks, "slab", scatter_dimension=0, tiled=True)
    mine = lax.all_to_all(mine.reshape(mine.shape[1:]), "ang", split_axis=0, concat_axis=0, tiled=True)
    real, imag = placed_columns(mine, jnp.asarray(placement(full_width, count_ang)), lax.axis_index("ang"))
    return (real.reshape(Z_DEV, KY, -1), imag.reshape(Z_DEV, KY, -1))


def solution(mesh):
    placed = (P("slab", "ang", None), P("slab", None), P("slab", None), P("slab", None))
    return jax.shard_map(
        on_device,
        mesh=mesh,
        in_specs=placed,
        out_specs=(P("slab", None, "ang"), P("slab", None, "ang")),
        check_vma=False,
    )
```

time: 500 us -> 144 us (0.29); the launches traced: 490 us -> 142 us
  other arithmetic: 248 us -> 0.28 us
  matrix products: 62.4 us -> 3.77 us
  local copies, waits for them, and re-layouts: 49.7 us -> 10.5 us
  Pallas kernels: 0 us -> 31 us
  waiting for transfers between devices: 101 us -> 74.9 us
  starting transfers between devices: 14.4 us -> 7.26 us
    scatter-add x6 -> x0, other arithmetic: 153 us -> none  [grid_rows(): buffer = buffer.at[index].add(weight[:, None] * rows)]
    convert_element_type x13 -> x1, other arithmetic: 70.4 us -> 0.04 us  [plane_weights(): weight = (jnp.exp(-0.5 * distance * distance) * density).astype(BF16)]
    dot_general x3 -> x1, matrix products: 62.4 us -> 3.77 us  [plane_weights(): return jnp.dot(update, spread, preferred_element_type=F32).astype(BF16)]
    pallas_call x0 -> x3, Pallas kernels: none -> 31 us  [the longest x1 24.5 us: gridded_blocks(): pl.pallas_call(functools.partial(grid_kernel, local_count, unitary), out_...]
    all_to_all x1 -> x2, waiting for transfers between devices: 45.9 us -> 25.5 us  [the longest x1 18.5 us: on_device(): lax.all_to_all(spectra, 'ang', split_axis=0, concat_axis=0, tiled=True)]
    all_to_all x1 -> x0, local copies, waits for them, and re-layouts: 20.1 us -> none  [on_device(): lax.all_to_all(row_spectra, 'ang', split_axis=3, concat_axis=1, tiled=True)]
    another operation x2 -> x0, other arithmetic: 11.7 us -> none  [the longest x1 9.07 us: on_device(): jnp.stack([transformed[:, :full_width], -transformed[:, full_width:]], ax...]
    add x1 -> x0, other arithmetic: 11.2 us -> none  [on_device(): real_part = cosine_part[:, :, :half_cols] + sine_part[:, :, half_cols:]]
  transfers between devices with their start and end apart: 6 -> 3, of which waited for: 4 -> 3; matrix products, arithmetic and copies ran while one was open for 0% -> 5% of each run, Pallas kernels for 0% -> 0%
where the time goes in v1:
time: 144 us; the launch traced here: 142 us
  waiting for transfers between devices  74.9 us (52%)
  Pallas kernels  31 us (22%)
  between operations  14.2 us (10%)
  local copies, waits for them, and re-layouts  10.5 us (7%)
  starting transfers between devices  7.26 us (5%)
  matrix products  3.77 us (3%)
    reduce_scatter x1, waiting for transfers between devices, on_device(): mine = lax.psum_scatter(blocks, 'slab', scatter_dimension=0, tiled=True)  49.4 us
    pallas_call x1, Pallas kernels, gridded_blocks(): pl.pallas_call(functools.partial(grid_kernel, local_count, unitary), out_...  24.5 us
    all_to_all x1, waiting for transfers between devices, on_device(): lax.all_to_all(spectra, 'ang', split_axis=0, concat_axis=0, tiled=True)  18.5 us
    unnamed x30, local copies, waits for them, and re-layouts  8.91 us
    all_to_all x1, waiting for transfers between devices, on_device(): lax.all_to_all(mine.reshape(mine.shape[1:]), 'ang', split_axis=0, concat_...  7.03 us
    pallas_call x1, Pallas kernels, column_spectra(): pl.pallas_call(columns_kernel, grid=(groups,), out_shape=jax.ShapeDtypeSt...  5.02 us
    dot_general x1, matrix products, plane_weights(): return jnp.dot(update, spread, preferred_element_type=F32).astype(BF16)  3.77 us
    all_to_all x1, starting transfers between devices, on_device(): lax.all_to_all(spectra, 'ang', split_axis=0, concat_axis=0, tiled=True)  3.75 us
  transfers between devices with their start and end apart: 3, of which 3 were waited for; matrix products, arithmetic and copies ran while one was open for 5% of the time, Pallas kernels for 0%

profile of v1, /device:TPU:17, one launch (start us, length us, event | category | flops | bytes accessed | tf_op | source)
XLA Modules:
  0.0 141.9 jit_solution(17726844953060057283)
XLA Ops:
  7.2 0.0 copy-start.1
  7.2 1.6 %copy-done.1 = bf16[2,256,2048]{2,1,0:T(8,128)(2,1)S(1)} copy-done((bf16[2,256,2048]{2,1,0:T(8,128)(2,1)S(1)}, bf16[2,256,2048]{2,1,0:T(8,128)(2,1)}, u32[]{:S(2)}) %copy-start.1) | copy-done | bytes 2097176
  8.8 0.0 copy-start.2
  8.8 3.4 %copy-done.2 = bf16[4,2048,512]{2,1,0:T(8,128)(2,1)S(1)} copy-done((bf16[4,2048,512]{2,1,0:T(8,128)(2,1)S(1)}, bf16[4,2048,512]{2,1,0:T(8,128)(2,1)}, u32[]{:S(2)}) %copy-start.2) | copy-done | bytes 8388632
  12.1 5.0 %shard_map.113 = bf16[4,512,512]{2,1,0:T(8,128)(2,1)S(1)} custom-call(bf16[512,2048]{1,0:T(8,128)(2,1)S(1)} %bitcast.37, bf16[4,2048,512]{2,1,0:T(8,128)(2,1)S(1)} %copy-done.2), custom_call_target="tpu_custom_call" | custom-call | flops 4294967296 | bytes 12582912 | tf_op jit(solution)/shard_map/pallas_call | solution.py:104
  17.2 0.0 copy-start
  17.2 1.4 copy-done
  18.5 0.0 copy-start.6
  18.5 0.0 copy-start.7
  18.5 0.0 copy-start.8
  18.5 0.0 slice-start.1
  18.5 0.0 slice-start.2
  18.6 0.0 copy-start.9
  18.6 3.8 %all-to-all-start = ((bf16[4,512,512]{2,1,0:T(8,128)(2,1)}), bf16[4,512,512]{2,1,0:T(8,128)(2,1)S(1)}, u32[]{:S(2)}, u32[]{:S(2)}) async-start(bf16[4,512,512]{2,1,0:T(8,128)(2,1)} %copy-done), calls=%async_computation | async-start | bytes 4194304 | tf_op jit(solution)/shard_map/all_to_all | solution.py:279
  22.3 0.0 reduce-scatter.2.cloned.1.call-start
  22.4 0.0 copy-done.6
  22.4 0.1 fusion.57
  22.5 0.0 copy-done.7
  22.5 0.1 fusion.59
  22.5 0.0 copy-done.8
  22.5 0.1 fusion.55
  22.6 0.4 reverse.1
  23.0 0.1 slice.82
  23.1 0.4 reverse
  23.4 0.1 slice.81
  23.5 0.4 reverse.2
  23.8 0.1 slice.83
  23.9 0.0 slice-done
  23.9 0.1 add_bitcast_fusion.2
  24.1 0.0 slice-done.1
  24.1 0.1 add_bitcast_fusion
  24.2 0.0 slice-done.2
  24.2 0.1 add_bitcast_fusion.4
  24.3 0.0 copy-done.9
  24.3 0.0 copy-start.3
  24.4 0.0 copy-start.5
  24.4 3.8 %fusion.v_ref = bf16[256,4096]{1,0:T(8,128)(2,1)} fusion(bf16[256,256]{1,0:T(8,128)(2,1)S(1)} %copy-done.9, s32[4096]{0:T(1024)S(1)} %bitcast.43, bf16[4096]{0:T(1024)(128)(2,1)S(1)} %get-tuple-element.11, bf16[4096]{0:T(1024)(128)(2,1)S(1)} %get-tuple-element.10, bf16[4096]{0:T(1024)(128)(2,1)S(1)} %get-tuple-element.9, ...), kind=kOutput, calls=%fused_computation.1 | convolution fusion | flops 551550976 | bytes 2293760 | tf_op jit(solution)/shard_map/dot_general | solution.py:266
  28.1 18.5 %all-to-all-done = bf16[4,512,512]{2,1,0:T(8,128)(2,1)S(1)} async-done(((bf16[4,512,512]{2,1,0:T(8,128)(2,1)}), bf16[4,512,512]{2,1,0:T(8,128)(2,1)S(1)}, u32[]{:S(2)}, u32[]{:S(2)}) %all-to-all-start) | async-done | bytes 2097184 | tf_op jit(solution)/shard_map/all_to_all | solution.py:279
  46.6 0.0 copy-done.3
  46.6 0.0 copy-done.5
  46.6 1.2 copy-done.4
  47.9 24.5 %shard_map.114 = bf16[8,4,256,256]{3,2,1,0:T(8,128)(2,1)} custom-call(s32[128]{0:T(128)S(1)} %copy-done.5, bf16[4,2,256,512]{3,2,1,0:T(8,128)(2,1)S(1)} %bitcast.36, bf16[512,1024]{1,0:T(8,128)(2,1)S(1)} %copy-done.3, bf16[512,1024]{1,0:T(8,128)(2,1)S(1)} %copy-done.4, bf16[256,4096]{1,0:T(8,128)(2,1)} %fusion.v_ref, s32[1,4096]{1,0:T(1,128)S(1)} %pad_add_fusion.1.ky_ref), custom_call_target="tpu_custom_call" | custom-call | flops 6442450944 | bytes 12582912 | tf_op jit(solution)/shard_map/pallas_call | solution.py:187
  72.4 0.0 reduce-scatter.2.cloned.1.call-update
  72.4 49.4 %reduce-scatter.2.cloned.1.call-done = bf16[1,4,256,256]{3,2,1,0:T(8,128)(2,1)} async-done(((bf16[8,4,256,256]{3,2,1,0:T(8,128)(2,1)}), bf16[1,4,256,256]{3,2,1,0:T(8,128)(2,1)}) %reduce-scatter.2.cloned.1.call-update) | async-done | bytes 524304 | tf_op jit(solution)/shard_map/reduce_scatter | solution.py:283
  121.8 3.5 %all-to-all-start.1 = ((bf16[4,256,256]{2,1,0:T(8,128)(2,1)}), bf16[4,256,256]{2,1,0:T(8,128)(2,1)S(1)}, u32[]{:S(2)}, u32[]{:S(2)}) async-start(bf16[4,256,256]{2,1,0:T(8,128)(2,1)} %bitcast.38), calls=%async_computation.2 | async-start | bytes 1048576 | tf_op jit(solution)/shard_map/all_to_all | solution.py:284
  125.3 1.3 constant_dynamic-slice_fusion.p_ref
  126.6 7.0 %all-to-all-done.1.x_ref = bf16[4,256,256]{2,1,0:T(8,128)(2,1)S(1)} async-done(((bf16[4,256,256]{2,1,0:T(8,128)(2,1)}), bf16[4,256,256]{2,1,0:T(8,128)(2,1)S(1)}, u32[]{:S(2)}, u32[]{:S(2)}) %all-to-all-start.1) | async-done | bytes 524320 | tf_op jit(solution)/shard_map/all_to_all | solution.py:284
  133.6 1.5 %shard_map.115 = (f32[256,512]{1,0:T(8,128)}, f32[256,512]{1,0:T(8,128)}) custom-call(bf16[4,256,256]{2,1,0:T(8,128)(2,1)S(1)} %all-to-all-done.1.x_ref, bf16[1,2,512,512]{3,2,1,0:T(8,128)(2,1)S(1)} %constant_dynamic-slice_fusion.p_ref), custom_call_target="tpu_custom_call" | custom-call | tf_op jit(solution)/shard_map/pallas_call | solution.py:241
  (13 shorter events, 0.1 us)
Async XLA Ops:
  7.2 1.6 %copy-start.1 = (bf16[2,256,2048]{2,1,0:T(8,128)(2,1)S(1)}, bf16[2,256,2048]{2,1,0:T(8,128)(2,1)}, u32[]{:S(2)}) copy-start(bf16[2,256,2048]{2,1,0:T(8,128)(2,1)} %param.10) | copy-start | bytes 6291460
  8.8 3.4 %copy-start.2 = (bf16[4,2048,512]{2,1,0:T(8,128)(2,1)S(1)}, bf16[4,2048,512]{2,1,0:T(8,128)(2,1)}, u32[]{:S(2)}) copy-start(bf16[4,2048,512]{2,1,0:T(8,128)(2,1)} %constant.52.clone.t_ref) | copy-start | bytes 25165828
  17.2 1.4 copy-start
  18.5 3.9 %copy-start.6 = (s32[2,1024]{1,0:T(2,128)S(1)}, s32[2,1024]{1,0:T(2,128)}, u32[]{:S(2)}) copy-start(s32[2,1024]{1,0:T(2,128)} %param.12) | copy-start | bytes 24580
  18.5 3.9 %copy-start.7 = (s32[2,1024]{1,0:T(2,128)S(1)}, s32[2,1024]{1,0:T(2,128)}, u32[]{:S(2)}) copy-start(s32[2,1024]{1,0:T(2,128)} %param.11) | copy-start | bytes 24580
  18.5 4.0 %copy-start.8 = (s32[2,1024]{1,0:T(2,128)S(1)}, s32[2,1024]{1,0:T(2,128)}, u32[]{:S(2)}) copy-start(s32[2,1024]{1,0:T(2,128)} %param.13) | copy-start | bytes 24580
  18.5 5.4 %slice-start = ((s32[2,1024]{1,0:T(2,128)}), s32[2,513]{1,0:T(2,128)S(1)}, s32[]{:S(2)}) async-start(s32[2,1024]{1,0:T(2,128)} %param.12), calls=%async_computation.4 | async-start | bytes 10240 | tf_op jit(solution)/shard_map/slice | solution.py:250
  18.5 5.5 %slice-start.1 = ((s32[2,1024]{1,0:T(2,128)}), s32[2,513]{1,0:T(2,128)S(1)}, s32[]{:S(2)}) async-start(s32[2,1024]{1,0:T(2,128)} %param.11), calls=%async_computation.5 | async-start | bytes 10240 | tf_op jit(solution)/shard_map/slice | solution.py:250
  18.5 5.6 %slice-start.2 = ((s32[2,1024]{1,0:T(2,128)}), s32[2,513]{1,0:T(2,128)S(1)}, s32[]{:S(2)}) async-start(s32[2,1024]{1,0:T(2,128)} %param.13), calls=%async_computation.6 | async-start | bytes 10240 | tf_op jit(solution)/shard_map/slice | solution.py:250
  18.6 5.8 %copy-start.9 = (bf16[256,256]{1,0:T(8,128)(2,1)S(1)}, bf16[256,256]{1,0:T(8,128)(2,1)}, u32[]{:S(2)}) copy-start(bf16[256,256]{1,0:T(8,128)(2,1)} %constant.53.clone) | copy-start | bytes 393220
  18.6 28.1 %all-to-all-start = ((bf16[4,512,512]{2,1,0:T(8,128)(2,1)}), bf16[4,512,512]{2,1,0:T(8,128)(2,1)S(1)}, u32[]{:S(2)}, u32[]{:S(2)}) async-start(bf16[4,512,512]{2,1,0:T(8,128)(2,1)} %copy-done), calls=%async_computation | async-start | bytes 4194304 | tf_op jit(solution)/shard_map/all_to_all | solution.py:279
  22.3 99.5 %reduce-scatter.2.cloned.1.call-start = ((), (), s32[]{:S(2)}) async-start(), calls=%async_computation.3 | async-start | bytes 4718592 | tf_op jit(solution)/shard_map/reduce_scatter | solution.py:283
  24.3 22.3 %copy-start.3 = (bf16[512,1024]{1,0:T(8,128)(2,1)S(1)}, bf16[512,1024]{1,0:T(8,128)(2,1)}, u32[]{:S(2)}) copy-start(bf16[512,1024]{1,0:T(8,128)(2,1)} %constant.55.clone.cos_ref) | copy-start | bytes 3145732
  24.4 22.3 %copy-start.5 = (s32[128]{0:T(128)S(1)}, s32[128]{0:T(128)}, u32[]{:S(2)}) copy-start(s32[128]{0:T(128)} %constant.54.clone.need_ref) | copy-start | bytes 1540
  46.6 1.2 copy-start.4
  121.8 11.8 %all-to-all-start.1 = ((bf16[4,256,256]{2,1,0:T(8,128)(2,1)}), bf16[4,256,256]{2,1,0:T(8,128)(2,1)S(1)}, u32[]{:S(2)}, u32[]{:S(2)}) async-start(bf16[4,256,256]{2,1,0:T(8,128)(2,1)} %bitcast.38), calls=%async_computation.2 | async-start | bytes 1048576 | tf_op jit(solution)/shard_map/all_to_all | solution.py:284
Sparse Core Ops, SparseCore 0:
  72.5 49.2 reduce-scatter.1

commit v2 on v1

--- a/solution.py
+++ b/solution.py
@@ -16,6 +16,7 @@
 SLOPE_LOW, SLOPE_HIGH = 8, 16
 CHUNK = 256
 BF16 = jnp.bfloat16
+MESH = pl.DeviceIdType.MESH
 F32 = jnp.float32
 
 
@@ -245,6 +246,387 @@
     )(received, lax.dynamic_slice_in_dim(table, me, 1, 0))
 
 
+def reach_of(rows, planes, height):
+    f = rows.astype(np.int64)
+    reach = [(64 * planes * f // (height * s)) // 8 + planes // 2 for s in range(SLOPE_LOW, SLOPE_HIGH + 1)]
+    low = max(int(np.min(reach)) - 2 - REG_ITERS, 0)
+    high = min(int(np.max(reach)) + 3 + REG_ITERS, planes - 1)
+    return low // Z_DEV, high // Z_DEV
+
+
+def chunk_reach(planes, height):
+    half = height // 2
+    negative = -np.arange(1, half)
+    up, down = np.arange(half), np.concatenate([[-half], negative])
+    mirror_up, mirror_down = np.concatenate([[0], negative]), np.concatenate([[-half], -negative])
+    table = []
+    for order in (np.concatenate([up, down]), np.concatenate([mirror_up, mirror_down])):
+        table.append([reach_of(order[i : i + CHUNK], planes, height) for i in range(0, height, CHUNK)])
+    return table
+
+
+def fused_kernel(
+    sizes,
+    x_ref,
+    table_ref,
+    cos_ref,
+    sin_ref,
+    update_ref,
+    place_ref,
+    index_ref,
+    real_ref,
+    imag_ref,
+    table,
+    place,
+    send_a,
+    recv_a,
+    weights,
+    acc_c,
+    acc_s,
+    spec_d,
+    spec_m,
+    acc_d,
+    acc_m,
+    pair_out,
+    pair_in,
+    total,
+    from_low,
+    from_high,
+    got,
+    table_sem,
+    place_sem,
+    a_send,
+    a_recv,
+    pair_send,
+    pair_recv,
+    line_send,
+    low_recv,
+    high_recv,
+    f_send,
+    f_recv,
+):
+    local_count, planes, chips, unitary, density = sizes
+    me = lax.axis_index("ang")
+    slab = lax.axis_index("slab")
+    z = slab // 2
+    core = slab % 2
+    half, height = cos_ref.shape
+    quarter_rows = height // 4
+    columns = recv_a.shape[-1]
+    quarter = columns // 4
+    chunks = height // CHUNK
+    peers = (3 - me, (me + 2) % 4, me + 1 - 2 * (me % 2), me)
+    other_core = slab + 1 - 2 * core
+
+    def table_copy(t):
+        return pltpu.make_async_copy(table_ref.at[peers[t]], table.at[t], table_sem.at[t])
+
+    place_copy = pltpu.make_async_copy(place_ref.at[me], place, place_sem)
+    for t in range(4):
+        table_copy(t).start()
+    place_copy.start()
+
+    barrier = pltpu.get_barrier_semaphore()
+    for t in range(3):
+        pl.semaphore_signal(barrier, inc=1, device_id={"ang": peers[t]}, device_id_type=MESH)
+    pl.semaphore_signal(barrier, inc=1, device_id={"slab": other_core}, device_id_type=MESH)
+
+    @pl.when(z > 0)
+    def _():
+        pl.semaphore_signal(barrier, inc=1, device_id={"slab": slab - 2}, device_id_type=MESH)
+
+    @pl.when(z < chips - 1)
+    def _():
+        pl.semaphore_signal(barrier, inc=1, device_id={"slab": slab + 2}, device_id_type=MESH)
+
+    at_end = jnp.logical_or(z == 0, z == chips - 1)
+
+    @pl.when(at_end)
+    def _():
+        pl.semaphore_wait(barrier, 5)
+
+    @pl.when(jnp.logical_not(at_end))
+    def _():
+        pl.semaphore_wait(barrier, 6)
+
+    def a_copy(t):
+        return pltpu.make_async_remote_copy(
+            src_ref=send_a.at[t],
+            dst_ref=recv_a.at[t],
+            send_sem=a_send.at[t],
+            recv_sem=a_recv.at[t],
+            device_id={"ang": peers[t]},
+            device_id_type=MESH,
+        )
+
+    for t in range(4):
+        table_copy(t).wait()
+        target = send_a if t < 3 else recv_a
+        target[t] = jnp.dot(x_ref[...], table[t], preferred_element_type=F32).astype(BF16)
+        if t < 3:
+            a_copy(t).start()
+
+    def weigh(i, carry):
+        at = pl.ds(pl.multiple_of(i * CHUNK, CHUNK), CHUNK)
+        shift = lax.broadcasted_iota(jnp.int32, (planes, CHUNK), 0) - index_ref[0:1, at]
+        eighth = index_ref[1:2, at].astype(F32) * 0.125
+        spread = jnp.zeros((planes, CHUNK), F32)
+        for g in range(-2, 4):
+            distance = g - eighth
+            weight = jnp.exp(-0.5 * distance * distance) * density
+            spread = jnp.where(shift == g, weight, spread)
+        value = jnp.dot(update_ref[...], spread.astype(BF16), preferred_element_type=F32)
+        weights[:, at] = value.astype(BF16)
+        return carry
+
+    lax.fori_loop(0, 2 * local_count * chunks, weigh, 0)
+
+    for t in (3, 2, 1, 0):
+        if t < 3:
+            a_copy(t).wait()
+        at = pl.ds(pl.multiple_of(peers[t] * quarter_rows, quarter_rows), quarter_rows)
+        for p in range(local_count):
+            rows = recv_a[t, p * quarter_rows : (p + 1) * quarter_rows, :]
+            for trig, acc in ((cos_ref, acc_c), (sin_ref, acc_s)):
+                term = jnp.dot(trig[:, at], rows, preferred_element_type=F32)
+                acc[p] = term if t == 3 else acc[p] + term
+
+    def finish(p, carry):
+        cosine, sine = acc_c[p], acc_s[p]
+        first = lax.broadcasted_iota(jnp.int32, (half, columns), 0) == 0
+        other = jnp.where(first, sine, cosine)
+        sine = jnp.where(first, 0.0, sine)
+        lane = lax.broadcasted_iota(jnp.int32, (half, quarter), 1)
+        packed = jnp.logical_and(lane == 0, me == 0)
+
+        def part(a, i):
+            return a[:, i * quarter : (i + 1) * quarter]
+
+        for sign, (c, s) in enumerate(((cosine, sine), (other, -sine))):
+            re0 = part(c, 0) + jnp.where(packed, 0.0, part(s, 2))
+            im0 = jnp.where(packed, 0.0, part(c, 2)) - part(s, 0)
+            re1 = part(c, 1) + part(s, 3)
+            im1 = part(c, 3) - part(s, 1)
+            re0m = jnp.where(packed, re1, re0)
+            im0m = jnp.where(packed, im1, im0)
+            re1m = jnp.where(packed, part(c, 2), re1)
+            im1m = jnp.where(packed, -part(s, 2), im1)
+            at = pl.ds(pl.multiple_of((p * 2 + sign) * half, half), half)
+            for i, value in enumerate((re0, im0, re1, im1)):
+                spec_d[at, i * quarter : (i + 1) * quarter] = (value * unitary).astype(BF16)
+            for i, value in enumerate((re1m, im1m, re0m, im0m)):
+                spec_m[at, i * quarter : (i + 1) * quarter] = (value * unitary).astype(BF16)
+        return carry
+
+    lax.fori_loop(0, local_count, finish, 0)
+
+    reach = chunk_reach(planes, height)
+    ky_row = lax.broadcasted_iota(jnp.int32, (KY, CHUNK), 0)
+
+    def compute(block):
+        acc_d[...] = jnp.zeros_like(acc_d)
+        acc_m[...] = jnp.zeros_like(acc_m)
+        plane = pl.ds(pl.multiple_of(block * Z_DEV, Z_DEV), Z_DEV)
+        for kind, (spec, acc) in enumerate(((spec_d, acc_d), (spec_m, acc_m))):
+            for c in range(local_count * chunks):
+                low, high = reach[kind][c % chunks]
+
+                @pl.when(jnp.logical_and(block >= low, block <= high))
+                def _(kind=kind, spec=spec, acc=acc, c=c):
+                    at = (kind * local_count * chunks + c) * CHUNK
+                    weight = weights[plane, at : at + CHUNK].astype(F32)
+                    hit = index_ref[2:3, at : at + CHUNK] == ky_row
+                    spread = jnp.where(hit[None], weight[:, None, :], 0.0)
+                    spread = spread.reshape(Z_DEV * KY, CHUNK).astype(BF16)
+                    acc[...] += jnp.dot(spread, spec[c * CHUNK : (c + 1) * CHUNK, :], preferred_element_type=F32)
+
+    def piece(i):
+        acc = (acc_d, acc_m)[i // 2]
+        return acc[:, (i % 2) * 2 * quarter : (i % 2 + 1) * 2 * quarter]
+
+    def order(t):
+        middle = jnp.where(t > 0, (t + 1) % 3 + 1, 0)
+        base = jnp.where(jnp.logical_or(z == 0, z == chips - 1), t, middle)
+        return jnp.where(z >= chips // 2, base, chips - 1 - base)
+
+    def pair_copy(t):
+        return pltpu.make_async_remote_copy(
+            src_ref=pair_out.at[t],
+            dst_ref=pair_in.at[t],
+            send_sem=pair_send.at[t],
+            recv_sem=pair_recv.at[t],
+            device_id={"slab": other_core},
+            device_id_type=MESH,
+        )
+
+    def line_copy(t, owner, up):
+        buffer, sem = (from_low, low_recv) if up else (from_high, high_recv)
+        return pltpu.make_async_remote_copy(
+            src_ref=total.at[t],
+            dst_ref=buffer.at[owner],
+            send_sem=line_send.at[t],
+            recv_sem=sem.at[owner],
+            device_id={"slab": slab + 2 if up else slab - 2},
+            device_id_type=MESH,
+        )
+
+    def add(t, buffer, owner):
+        total[t] = (total[t].astype(F32) + buffer[owner].astype(F32)).astype(BF16)
+
+    def forward(t):
+        owner = order(t)
+
+        @pl.when(owner > z)
+        def _():
+            @pl.when(z > 0)
+            def _():
+                line_copy(t, owner, True).wait_recv()
+                add(t, from_low, owner)
+
+            line_copy(t, owner, True).start()
+
+        @pl.when(owner < z)
+        def _():
+            @pl.when(z < chips - 1)
+            def _():
+                line_copy(t, owner, False).wait_recv()
+                add(t, from_high, owner)
+
+            line_copy(t, owner, False).start()
+
+    def step(t, carry):
+        owner = order(t)
+        compute(owner * 2 + 1 - core)
+        for i in range(4):
+            pair_out[t, i] = piece(i).astype(BF16)
+        pair_copy(t).start()
+        compute(owner * 2 + core)
+        pair_copy(t).wait_recv()
+        for i in range(4):
+            total[t, i] = (piece(i) + pair_in[t, i].astype(F32)).astype(BF16)
+
+        @pl.when(jnp.logical_and(at_end, t < chips - 1))
+        def _():
+            forward(t)
+
+        @pl.when(jnp.logical_and(jnp.logical_not(at_end), t > 0))
+        def _():
+            forward(t - 1)
+
+        return carry
+
+    lax.fori_loop(0, chips, step, 0)
+
+    last = chips - 1
+
+    @pl.when(z > 0)
+    def _():
+        line_copy(last, z, True).wait_recv()
+        add(last, from_low, z)
+
+    @pl.when(z < chips - 1)
+    def _():
+        line_copy(last, z, False).wait_recv()
+        add(last, from_high, z)
+
+    def f_copy(t):
+        return pltpu.make_async_remote_copy(
+            src_ref=total.at[last, peers[t]],
+            dst_ref=got.at[t],
+            send_sem=f_send.at[t],
+            recv_sem=f_recv.at[t],
+            device_id={"ang": peers[t]},
+            device_id_type=MESH,
+        )
+
+    for t in range(3):
+        f_copy(t).start()
+    place_copy.wait()
+    for t in (3, 2, 1, 0):
+        if t < 3:
+            f_copy(t).wait()
+        value = total[last, me] if t == 3 else got[t]
+        at = pl.ds(pl.multiple_of(peers[t] * quarter, quarter), quarter)
+        for i, out in enumerate((real_ref, imag_ref)):
+            term = jnp.dot(value[:, i * quarter : (i + 1) * quarter], place[i, at, :], preferred_element_type=F32)
+            if t == 3:
+                out[...] = term
+            else:
+                out[...] += term
+
+    def drain(t, carry):
+        pair_copy(t).wait_send()
+
+        @pl.when(t < last)
+        def _():
+            line_copy(t, 0, True).wait_send()
+
+        return carry
+
+    lax.fori_loop(0, chips, drain, 0)
+
+
+def fused(rows, indices, local_count, planes, chips, height, unitary, density):
+    count, width = rows.shape
+    table = jnp.asarray(column_table(width, 4))
+    columns = table.shape[-1]
+    cosines, sines = row_tables(height)
+    places = jnp.asarray(placement(width, 4))
+    block = (4, Z_DEV * KY, columns // 2)
+    slots = local_count * height
+    vmem = pl.BlockSpec(memory_space=pltpu.VMEM)
+    anywhere = pl.BlockSpec(memory_space=pl.ANY)
+    dma = pltpu.SemaphoreType.DMA
+    return pl.pallas_call(
+        functools.partial(fused_kernel, (local_count, planes, chips, unitary, density)),
+        out_shape=[jax.ShapeDtypeStruct((Z_DEV * KY, width // 4), F32)] * 2,
+        in_specs=[vmem, anywhere, vmem, vmem, vmem, anywhere, vmem],
+        out_specs=[vmem, vmem],
+        scratch_shapes=[
+            pltpu.VMEM(table.shape, BF16),
+            pltpu.VMEM(places.shape[1:], BF16),
+            pltpu.VMEM((3, count, columns), BF16),
+            pltpu.VMEM((4, count, columns), BF16),
+            pltpu.VMEM((planes, 2 * slots), BF16),
+            pltpu.VMEM((local_count, height // 2, columns), F32),
+            pltpu.VMEM((local_count, height // 2, columns), F32),
+            pltpu.VMEM((slots, columns), BF16),
+            pltpu.VMEM((slots, columns), BF16),
+            pltpu.VMEM((Z_DEV * KY, columns), F32),
+            pltpu.VMEM((Z_DEV * KY, columns), F32),
+            pltpu.VMEM((chips,) + block, BF16),
+            pltpu.VMEM((chips,) + block, BF16),
+            pltpu.VMEM((chips,) + block, BF16),
+            pltpu.VMEM((chips,) + block, BF16),
+            pltpu.VMEM((chips,) + block, BF16),
+            pltpu.VMEM((3,) + block[1:], BF16),
+            dma((4,)),
+            dma,
+            dma((3,)),
+            dma((3,)),
+            dma((chips,)),
+            dma((chips,)),
+            dma((chips,)),
+            dma((chips,)),
+            dma((chips,)),
+            dma((3,)),
+            dma((3,)),
+        ],
+        compiler_params=pltpu.CompilerParams(
+            collective_id=0, has_side_effects=True, vmem_limit_bytes=58 * 2**20
+        ),
+        cost_estimate=pl.CostEstimate(flops=14 * 10**9, bytes_accessed=20 * 2**20, transcendentals=0),
+    )(
+        rows,
+        table,
+        jnp.asarray(cosines),
+        jnp.asarray(sines),
+        jnp.asarray(update_matrix(planes)),
+        places,
+        indices,
+    )
+
+
 def slot_orders(values):
     half = values.shape[1] // 2
     low, high = values[:, :half], values[:, half:]
@@ -274,6 +656,19 @@
     planes = Z_DEV * count_slab
     unitary = 1.0 / math.sqrt(height * full_width)
     density = 1.0 / math.sqrt(local_count * count_slab)
+    if count_ang == 4 and count_slab == 8:
+        indices = jnp.concatenate([slot_orders(dest_plane), slot_orders(sub_offset), slot_orders(ky_bin)], axis=0)
+        real, imag = fused(
+            projections.reshape(local_count * quarter, full_width),
+            indices,
+            local_count,
+            planes,
+            count_slab // 2,
+            height,
+            unitary,
+            density,
+        )
+        return (real.reshape(Z_DEV, KY, -1), imag.reshape(Z_DEV, KY, -1))
     table = jnp.asarray(column_table(full_width, count_ang))
     spectra = column_spectra(projections.reshape(local_count * quarter, full_width), table)
     received = lax.all_to_all(spectra, "ang", split_axis=0, concat_axis=0, tiled=True)

time: 144 us -> 105 us (0.73)
  waiting for transfers between devices: 74.9 us -> 0 us
  Pallas kernels: 31 us -> 91 us
  between operations: 14.2 us -> 0.69 us
  starting transfers between devices: 7.26 us -> 0 us
  matrix products: 3.77 us -> 0 us
    pallas_call x3 -> x1, Pallas kernels: 31 us -> 91 us  [fused(): pl.pallas_call(functools.partial(fused_kernel, (local_count, planes, chip...]
    reduce_scatter x1 -> x0, waiting for transfers between devices: 49.4 us -> none  [on_device(): mine = lax.psum_scatter(blocks, 'slab', scatter_dimension=0, tiled=True)]
    all_to_all x2 -> x0, waiting for transfers between devices: 25.5 us -> none  [the longest x1 18.5 us: on_device(): lax.all_to_all(spectra, 'ang', split_axis=0, concat_axis=0, tiled=True)]
    all_to_all x2 -> x0, starting transfers between devices: 7.22 us -> none  [the longest x1 3.75 us: on_device(): lax.all_to_all(spectra, 'ang', split_axis=0, concat_axis=0, tiled=True)]
    unnamed x30 -> x14, local copies, waits for them, and re-layouts: 8.91 us -> 5.11 us
    dot_general x1 -> x0, matrix products: 3.77 us -> none  [plane_weights(): return jnp.dot(update, spread, preferred_element_type=F32).astype(BF16)]
    slice x3, local copies, waits for them, and re-layouts: 0.23 us -> 2.52 us  [slot_orders(): back_high = high[:, :0:-1]]
    slice x3, local copies, waits for them, and re-layouts: 0.01 us -> 2.09 us  [slot_orders(): low[:, :1]]
  transfers between devices with their start and end apart: 3 -> 0, of which waited for: 3 -> 0; matrix products, arithmetic and copies ran while one was open for 5% -> 0% of each run, Pallas kernels for 0% -> 0%
where the time goes in v2:
time: 105 us; the launch traced here: 104 us
  Pallas kernels  91 us (87%)
  local copies, waits for them, and re-layouts  11.8 us (11%)
    pallas_call x1, Pallas kernels, fused(): pl.pallas_call(functools.partial(fused_kernel, (local_count, planes, chip...  91 us
    unnamed x14, local copies, waits for them, and re-layouts  5.11 us
    slice x3, local copies, waits for them, and re-layouts, slot_orders(): back_high = high[:, :0:-1]  2.52 us

profile of v2, /device:TPU:17, one launch (start us, length us, event | category | flops | bytes accessed | tf_op | source)
XLA Modules:
  0.0 104.4 jit_solution(1779387618382524559)
XLA Ops:
  0.6 0.7 fusion
  1.3 0.7 fusion.2
  2.0 0.7 fusion.4
  2.7 0.7 slice.66
  3.4 0.7 slice.71
  4.1 0.7 slice.76
  4.8 0.8 fusion.1
  5.6 0.4 reverse.2
  6.0 0.1 slice.83
  6.1 0.1 add_bitcast_fusion
  6.2 0.8 fusion.3
  7.0 0.4 reverse.1
  7.4 0.1 slice.82
  7.5 0.1 add_bitcast_fusion.2
  7.6 0.8 fusion.5
  8.4 0.4 reverse
  8.8 0.1 slice.81
  8.9 0.1 add_bitcast_fusion.4
  9.0 0.7 add_add_fusion.index_ref
  9.7 91.0 %shard_map.104 = (f32[256,512]{1,0:T(8,128)}, f32[256,512]{1,0:T(8,128)}) custom-call(bf16[512,2048]{1,0:T(8,128)(2,1)} %bitcast.41, bf16[4,2048,512]{2,1,0:T(8,128)(2,1)} %constant.10.clone.table_ref, bf16[512,1024]{1,0:T(8,128)(2,1)} %constant.12.clone.cos_ref, bf16[512,1024]{1,0:T(8,128)(2,1)} %constant.13.clone.sin_ref, ...), custom_call_target="tpu_custom_call" | custom-call | flops 14000000000 | bytes 20971520 | tf_op jit(solution)/shard_map/pallas_call | solution.py:580
  100.6 1.9 %copy.19 = f32[32,8,512]{2,1,0:T(8,128)} copy(f32[32,8,512]{2,1,0:T(8,128)} %bitcast.31) | data formatting | bytes 1048576
  102.5 1.9 %copy.20 = f32[32,8,512]{2,1,0:T(8,128)} copy(f32[32,8,512]{2,1,0:T(8,128)} %bitcast.30) | data formatting | bytes 1048576
  (6 shorter events, 0.1 us)

commit v3 on v2

--- a/solution.py
+++ b/solution.py
@@ -246,25 +246,6 @@
     )(received, lax.dynamic_slice_in_dim(table, me, 1, 0))
 
 
-def reach_of(rows, planes, height):
-    f = rows.astype(np.int64)
-    reach = [(64 * planes * f // (height * s)) // 8 + planes // 2 for s in range(SLOPE_LOW, SLOPE_HIGH + 1)]
-    low = max(int(np.min(reach)) - 2 - REG_ITERS, 0)
-    high = min(int(np.max(reach)) + 3 + REG_ITERS, planes - 1)
-    return low // Z_DEV, high // Z_DEV
-
-
-def chunk_reach(planes, height):
-    half = height // 2
-    negative = -np.arange(1, half)
-    up, down = np.arange(half), np.concatenate([[-half], negative])
-    mirror_up, mirror_down = np.concatenate([[0], negative]), np.concatenate([[-half], -negative])
-    table = []
-    for order in (np.concatenate([up, down]), np.concatenate([mirror_up, mirror_down])):
-        table.append([reach_of(order[i : i + CHUNK], planes, height) for i in range(0, height, CHUNK)])
-    return table
-
-
 def fused_kernel(
     sizes,
     x_ref,
@@ -272,12 +253,12 @@
     cos_ref,
     sin_ref,
     update_ref,
-    place_ref,
+    dest_ref,
+    eighth_ref,
+    ky_ref,
+    out_ref,
+    table,
     index_ref,
-    real_ref,
-    imag_ref,
-    table,
-    place,
     send_a,
     recv_a,
     weights,
@@ -285,16 +266,15 @@
     acc_s,
     spec_d,
     spec_m,
-    acc_d,
-    acc_m,
+    spread,
     pair_out,
     pair_in,
     total,
     from_low,
     from_high,
+    own,
     got,
     table_sem,
-    place_sem,
     a_send,
     a_recv,
     pair_send,
@@ -321,10 +301,8 @@
     def table_copy(t):
         return pltpu.make_async_copy(table_ref.at[peers[t]], table.at[t], table_sem.at[t])
 
-    place_copy = pltpu.make_async_copy(place_ref.at[me], place, place_sem)
     for t in range(4):
         table_copy(t).start()
-    place_copy.start()
 
     barrier = pltpu.get_barrier_semaphore()
     for t in range(3):
@@ -366,17 +344,50 @@
         if t < 3:
             a_copy(t).start()
 
+    held = 8
+    raw = jnp.concatenate([dest_ref[...], eighth_ref[...], ky_ref[...]], axis=0)
+    raw = jnp.concatenate([raw, jnp.zeros((held - raw.shape[0], height), jnp.int32)], axis=0)
+    low, high = raw[:, :half], raw[:, half:]
+    row = lax.broadcasted_iota(jnp.int32, (half, half), 0)
+    flip = (row + lax.broadcasted_iota(jnp.int32, (half, half), 1) == half).astype(F32).astype(BF16)
+    back = jnp.dot(high.astype(F32).astype(BF16), flip, preferred_element_type=F32).astype(jnp.int32)
+    lane_0 = lax.broadcasted_iota(jnp.int32, (held, half), 1) == 0
+    low_0 = jnp.broadcast_to(low[:, :1], low.shape)
+    high_0 = jnp.broadcast_to(high[:, :1], high.shape)
+    orders = (
+        low,
+        jnp.where(lane_0, high_0, back),
+        jnp.where(lane_0, low_0, back),
+        jnp.where(lane_0, high_0, low),
+    )
+    for kind in range(2):
+        for p in range(local_count):
+            for sign in range(2):
+                at = ((kind * local_count + p) * 2 + sign) * half
+                for i in range(3):
+                    source = i * local_count + p
+                    index_ref[i : i + 1, at : at + half] = orders[kind * 2 + sign][source : source + 1, :]
+
     def weigh(i, carry):
         at = pl.ds(pl.multiple_of(i * CHUNK, CHUNK), CHUNK)
         shift = lax.broadcasted_iota(jnp.int32, (planes, CHUNK), 0) - index_ref[0:1, at]
         eighth = index_ref[1:2, at].astype(F32) * 0.125
-        spread = jnp.zeros((planes, CHUNK), F32)
+        window = jnp.zeros((planes, CHUNK), F32)
         for g in range(-2, 4):
             distance = g - eighth
             weight = jnp.exp(-0.5 * distance * distance) * density
-            spread = jnp.where(shift == g, weight, spread)
-        value = jnp.dot(update_ref[...], spread.astype(BF16), preferred_element_type=F32)
-        weights[:, at] = value.astype(BF16)
+            window = jnp.where(shift == g, weight, window)
+        value = jnp.dot(update_ref[...], window.astype(BF16), preferred_element_type=F32)
+        weights[...] = value
+        hit = index_ref[2:3, at] == lax.broadcasted_iota(jnp.int32, (KY, CHUNK), 0)
+
+        def scatter(block, inner):
+            plane = pl.ds(pl.multiple_of(block * Z_DEV, Z_DEV), Z_DEV)
+            cells = jnp.where(hit[None], weights[plane, :][:, None, :], 0.0)
+            spread[block, :, at] = cells.reshape(Z_DEV * KY, CHUNK).astype(BF16)
+            return inner
+
+        lax.fori_loop(0, planes // Z_DEV, scatter, 0)
         return carry
 
     lax.fori_loop(0, 2 * local_count * chunks, weigh, 0)
@@ -420,29 +431,16 @@
 
     lax.fori_loop(0, local_count, finish, 0)
 
-    reach = chunk_reach(planes, height)
-    ky_row = lax.broadcasted_iota(jnp.int32, (KY, CHUNK), 0)
-
-    def compute(block):
-        acc_d[...] = jnp.zeros_like(acc_d)
-        acc_m[...] = jnp.zeros_like(acc_m)
-        plane = pl.ds(pl.multiple_of(block * Z_DEV, Z_DEV), Z_DEV)
-        for kind, (spec, acc) in enumerate(((spec_d, acc_d), (spec_m, acc_m))):
-            for c in range(local_count * chunks):
-                low, high = reach[kind][c % chunks]
-
-                @pl.when(jnp.logical_and(block >= low, block <= high))
-                def _(kind=kind, spec=spec, acc=acc, c=c):
-                    at = (kind * local_count * chunks + c) * CHUNK
-                    weight = weights[plane, at : at + CHUNK].astype(F32)
-                    hit = index_ref[2:3, at : at + CHUNK] == ky_row
-                    spread = jnp.where(hit[None], weight[:, None, :], 0.0)
-                    spread = spread.reshape(Z_DEV * KY, CHUNK).astype(BF16)
-                    acc[...] += jnp.dot(spread, spec[c * CHUNK : (c + 1) * CHUNK, :], preferred_element_type=F32)
-
-    def piece(i):
-        acc = (acc_d, acc_m)[i // 2]
-        return acc[:, (i % 2) * 2 * quarter : (i % 2 + 1) * 2 * quarter]
+    slots = local_count * height
+
+    def piece(block, i):
+        kind, side = i // 2, i % 2
+        spec = (spec_d, spec_m)[kind]
+        return jnp.dot(
+            spread[block, :, kind * slots : (kind + 1) * slots],
+            spec[:, side * 2 * quarter : (side + 1) * 2 * quarter],
+            preferred_element_type=F32,
+        )
 
     def order(t):
         middle = jnp.where(t > 0, (t + 1) % 3 + 1, 0)
@@ -496,14 +494,14 @@
 
     def step(t, carry):
         owner = order(t)
-        compute(owner * 2 + 1 - core)
         for i in range(4):
-            pair_out[t, i] = piece(i).astype(BF16)
+            pair_out[t, i] = piece(owner * 2 + 1 - core, i).astype(BF16)
         pair_copy(t).start()
-        compute(owner * 2 + core)
+        for i in range(4):
+            own[i] = piece(owner * 2 + core, i)
         pair_copy(t).wait_recv()
         for i in range(4):
-            total[t, i] = (piece(i) + pair_in[t, i].astype(F32)).astype(BF16)
+            total[t, i] = (own[i] + pair_in[t, i].astype(F32)).astype(BF16)
 
         @pl.when(jnp.logical_and(at_end, t < chips - 1))
         def _():
@@ -541,18 +539,10 @@
 
     for t in range(3):
         f_copy(t).start()
-    place_copy.wait()
-    for t in (3, 2, 1, 0):
-        if t < 3:
-            f_copy(t).wait()
-        value = total[last, me] if t == 3 else got[t]
-        at = pl.ds(pl.multiple_of(peers[t] * quarter, quarter), quarter)
-        for i, out in enumerate((real_ref, imag_ref)):
-            term = jnp.dot(value[:, i * quarter : (i + 1) * quarter], place[i, at, :], preferred_element_type=F32)
-            if t == 3:
-                out[...] = term
-            else:
-                out[...] += term
+    out_ref[3] = total[last, me]
+    for t in range(3):
+        f_copy(t).wait()
+        out_ref[t] = got[t]
 
     def drain(t, carry):
         pair_copy(t).wait_send()
@@ -566,12 +556,11 @@
     lax.fori_loop(0, chips, drain, 0)
 
 
-def fused(rows, indices, local_count, planes, chips, height, unitary, density):
+def fused(rows, dest, eighths, ky, local_count, planes, chips, height, unitary, density):
     count, width = rows.shape
     table = jnp.asarray(column_table(width, 4))
     columns = table.shape[-1]
     cosines, sines = row_tables(height)
-    places = jnp.asarray(placement(width, 4))
     block = (4, Z_DEV * KY, columns // 2)
     slots = local_count * height
     vmem = pl.BlockSpec(memory_space=pltpu.VMEM)
@@ -579,29 +568,28 @@
     dma = pltpu.SemaphoreType.DMA
     return pl.pallas_call(
         functools.partial(fused_kernel, (local_count, planes, chips, unitary, density)),
-        out_shape=[jax.ShapeDtypeStruct((Z_DEV * KY, width // 4), F32)] * 2,
-        in_specs=[vmem, anywhere, vmem, vmem, vmem, anywhere, vmem],
-        out_specs=[vmem, vmem],
+        out_shape=jax.ShapeDtypeStruct(block, BF16),
+        in_specs=[vmem, anywhere, vmem, vmem, vmem, vmem, vmem, vmem],
+        out_specs=vmem,
         scratch_shapes=[
             pltpu.VMEM(table.shape, BF16),
-            pltpu.VMEM(places.shape[1:], BF16),
+            pltpu.VMEM((8, 2 * slots), jnp.int32),
             pltpu.VMEM((3, count, columns), BF16),
             pltpu.VMEM((4, count, columns), BF16),
-            pltpu.VMEM((planes, 2 * slots), BF16),
+            pltpu.VMEM((planes, CHUNK), F32),
             pltpu.VMEM((local_count, height // 2, columns), F32),
             pltpu.VMEM((local_count, height // 2, columns), F32),
             pltpu.VMEM((slots, columns), BF16),
             pltpu.VMEM((slots, columns), BF16),
-            pltpu.VMEM((Z_DEV * KY, columns), F32),
-            pltpu.VMEM((Z_DEV * KY, columns), F32),
+            pltpu.VMEM((planes // Z_DEV, Z_DEV * KY, 2 * slots), BF16),
             pltpu.VMEM((chips,) + block, BF16),
             pltpu.VMEM((chips,) + block, BF16),
             pltpu.VMEM((chips,) + block, BF16),
             pltpu.VMEM((chips,) + block, BF16),
             pltpu.VMEM((chips,) + block, BF16),
+            pltpu.VMEM(block, F32),
             pltpu.VMEM((3,) + block[1:], BF16),
             dma((4,)),
-            dma,
             dma((3,)),
             dma((3,)),
             dma((chips,)),
@@ -622,9 +610,39 @@
         jnp.asarray(cosines),
         jnp.asarray(sines),
         jnp.asarray(update_matrix(planes)),
-        places,
-        indices,
+        dest,
+        eighths,
+        ky,
     )
+
+
+def gathered_kernel(x_ref, place_ref, real_ref, imag_ref, place, sem):
+    me = lax.axis_index("ang")
+    copy = pltpu.make_async_copy(place_ref.at[me], place, sem)
+    copy.start()
+    peers = (3 - me, (me + 2) % 4, me + 1 - 2 * (me % 2), me)
+    half = x_ref.shape[-1] // 2
+    copy.wait()
+    for i, out in enumerate((real_ref, imag_ref)):
+        total = None
+        for t in range(4):
+            at = pl.ds(pl.multiple_of(peers[t] * half, half), half)
+            term = jnp.dot(x_ref[t, :, i * half : (i + 1) * half], place[i, at, :], preferred_element_type=F32)
+            total = term if total is None else total + term
+        out[...] = total
+
+
+def gathered_columns(received, table):
+    rows, block = received.shape[1], table.shape[-1]
+    vmem = pl.BlockSpec(memory_space=pltpu.VMEM)
+    return pl.pallas_call(
+        gathered_kernel,
+        out_shape=[jax.ShapeDtypeStruct((rows, block), F32)] * 2,
+        in_specs=[vmem, pl.BlockSpec(memory_space=pl.ANY)],
+        out_specs=[vmem, vmem],
+        scratch_shapes=[pltpu.VMEM(table.shape[1:], BF16), pltpu.SemaphoreType.DMA],
+        compiler_params=pltpu.CompilerParams(vmem_limit_bytes=40 * 2**20),
+    )(received, table)
 
 
 def slot_orders(values):
@@ -657,10 +675,11 @@
     unitary = 1.0 / math.sqrt(height * full_width)
     density = 1.0 / math.sqrt(local_count * count_slab)
     if count_ang == 4 and count_slab == 8:
-        indices = jnp.concatenate([slot_orders(dest_plane), slot_orders(sub_offset), slot_orders(ky_bin)], axis=0)
-        real, imag = fused(
+        mine = fused(
             projections.reshape(local_count * quarter, full_width),
-            indices,
+            dest_plane,
+            sub_offset,
+            ky_bin,
             local_count,
             planes,
             count_slab // 2,
@@ -668,6 +687,7 @@
             unitary,
             density,
         )
+        real, imag = gathered_columns(mine, jnp.asarray(placement(full_width, count_ang)))
         return (real.reshape(Z_DEV, KY, -1), imag.reshape(Z_DEV, KY, -1))
     table = jnp.asarray(column_table(full_width, count_ang))
     spectra = column_spectra(projections.reshape(local_count * quarter, full_width), table)

time: 105 us -> 93.5 us (0.89)
  local copies, waits for them, and re-layouts: 11.8 us -> 1.04 us
    slice x9 -> x0, local copies, waits for them, and re-layouts: 6.68 us -> none  [the longest x3 2.52 us: slot_orders(): back_high = high[:, :0:-1]]
    unnamed x14 -> x4, local copies, waits for them, and re-layouts: 5.11 us -> 1.04 us
    pallas_call x0 -> x1, Pallas kernels: none -> 1.56 us  [gathered_columns(): pl.pallas_call(gathered_kernel, out_shape=[jax.ShapeDtypeStruct((rows, bl...]
where the time goes in v3:
time: 93.5 us; the launch traced here: 93.3 us
  Pallas kernels  91.6 us (98%)
  local copies, waits for them, and re-layouts  1.04 us (1%)
    pallas_call x1, Pallas kernels, fused(): pl.pallas_call(functools.partial(fused_kernel, (local_count, planes, chip...  90.1 us

profile of v3, /device:TPU:17, one launch (start us, length us, event | category | flops | bytes accessed | tf_op | source)
XLA Modules:
  0.0 93.3 jit_solution(835759339731495361)
XLA Ops:
  0.6 0.0 copy-start
  0.6 90.1 %shard_map.104.x_ref = bf16[4,256,256]{2,1,0:T(8,128)(2,1)} custom-call(bf16[512,2048]{1,0:T(8,128)(2,1)} %bitcast.3, bf16[4,2048,512]{2,1,0:T(8,128)(2,1)} %constant.10.clone.table_ref, bf16[512,1024]{1,0:T(8,128)(2,1)} %constant.11.clone.cos_ref, bf16[512,1024]{1,0:T(8,128)(2,1)} %constant.12.clone.sin_ref, bf16[256,256]{1,0:T(8,128)(2,1)} %constant.13.clone.update_ref, ...), custom_call_target="tpu_custom_call" | custom-call | flops 14000000000 | bytes 20971520 | tf_op jit(solution)/shard_map/pallas_call | solution.py:569
  90.7 0.0 copy-done
  90.7 0.0 copy-start.1
  90.7 1.0 %copy-done.1 = bf16[4,256,256]{2,1,0:T(8,128)(2,1)S(1)} copy-done((bf16[4,256,256]{2,1,0:T(8,128)(2,1)S(1)}, bf16[4,256,256]{2,1,0:T(8,128)(2,1)}, u32[]{:S(2)}) %copy-start.1) | copy-done | bytes 524312
  91.8 1.6 %shard_map.105 = (f32[256,512]{1,0:T(8,128)}, f32[256,512]{1,0:T(8,128)}) custom-call(bf16[4,256,256]{2,1,0:T(8,128)(2,1)S(1)} %copy-done.1, bf16[4,2,512,512]{3,2,1,0:T(8,128)(2,1)S(1)} %copy-done), custom_call_target="tpu_custom_call" | custom-call | tf_op jit(solution)/shard_map/pallas_call | solution.py:638
Async XLA Ops:
  0.6 90.1 %copy-start = (bf16[4,2,512,512]{3,2,1,0:T(8,128)(2,1)S(1)}, bf16[4,2,512,512]{3,2,1,0:T(8,128)(2,1)}, u32[]{:S(2)}) copy-start(bf16[4,2,512,512]{3,2,1,0:T(8,128)(2,1)} %constant.14.clone.place_ref) | copy-start | bytes 12582916
  90.7 1.0 %copy-start.1 = (bf16[4,256,256]{2,1,0:T(8,128)(2,1)S(1)}, bf16[4,256,256]{2,1,0:T(8,128)(2,1)}, u32[]{:S(2)}) copy-start(bf16[4,256,256]{2,1,0:T(8,128)(2,1)} %shard_map.104.x_ref) | copy-start | bytes 1572868

commit v4 on v3

--- a/solution.py
+++ b/solution.py
@@ -457,40 +457,44 @@
             device_id_type=MESH,
         )
 
-    def line_copy(t, owner, up):
+    def line_copy(t, owner, up, i):
         buffer, sem = (from_low, low_recv) if up else (from_high, high_recv)
         return pltpu.make_async_remote_copy(
-            src_ref=total.at[t],
-            dst_ref=buffer.at[owner],
-            send_sem=line_send.at[t],
-            recv_sem=sem.at[owner],
+            src_ref=total.at[t, i],
+            dst_ref=buffer.at[owner, i],
+            send_sem=line_send.at[t, i],
+            recv_sem=sem.at[owner, i],
             device_id={"slab": slab + 2 if up else slab - 2},
             device_id_type=MESH,
         )
 
-    def add(t, buffer, owner):
-        total[t] = (total[t].astype(F32) + buffer[owner].astype(F32)).astype(BF16)
+    def add(t, buffer, owner, i):
+        total[t, i] = (total[t, i].astype(F32) + buffer[owner, i].astype(F32)).astype(BF16)
 
     def forward(t):
         owner = order(t)
 
         @pl.when(owner > z)
         def _():
-            @pl.when(z > 0)
-            def _():
-                line_copy(t, owner, True).wait_recv()
-                add(t, from_low, owner)
-
-            line_copy(t, owner, True).start()
+            for i in peers:
+
+                @pl.when(z > 0)
+                def _():
+                    line_copy(t, owner, True, i).wait_recv()
+                    add(t, from_low, owner, i)
+
+                line_copy(t, owner, True, i).start()
 
         @pl.when(owner < z)
         def _():
-            @pl.when(z < chips - 1)
-            def _():
-                line_copy(t, owner, False).wait_recv()
-                add(t, from_high, owner)
-
-            line_copy(t, owner, False).start()
+            for i in peers:
+
+                @pl.when(z < chips - 1)
+                def _():
+                    line_copy(t, owner, False, i).wait_recv()
+                    add(t, from_high, owner, i)
+
+                line_copy(t, owner, False, i).start()
 
     def step(t, carry):
         owner = order(t)
@@ -517,16 +521,6 @@
 
     last = chips - 1
 
-    @pl.when(z > 0)
-    def _():
-        line_copy(last, z, True).wait_recv()
-        add(last, from_low, z)
-
-    @pl.when(z < chips - 1)
-    def _():
-        line_copy(last, z, False).wait_recv()
-        add(last, from_high, z)
-
     def f_copy(t):
         return pltpu.make_async_remote_copy(
             src_ref=total.at[last, peers[t]],
@@ -537,8 +531,21 @@
             device_id_type=MESH,
         )
 
-    for t in range(3):
-        f_copy(t).start()
+    for t in range(4):
+        i = peers[t]
+
+        @pl.when(z > 0)
+        def _():
+            line_copy(last, z, True, i).wait_recv()
+            add(last, from_low, z, i)
+
+        @pl.when(z < chips - 1)
+        def _():
+            line_copy(last, z, False, i).wait_recv()
+            add(last, from_high, z, i)
+
+        if t < 3:
+            f_copy(t).start()
     out_ref[3] = total[last, me]
     for t in range(3):
         f_copy(t).wait()
@@ -549,7 +556,8 @@
 
         @pl.when(t < last)
         def _():
-            line_copy(t, 0, True).wait_send()
+            for i in range(4):
+                line_copy(t, 0, True, i).wait_send()
 
         return carry
 
@@ -594,9 +602,9 @@
             dma((3,)),
             dma((chips,)),
             dma((chips,)),
-            dma((chips,)),
-            dma((chips,)),
-            dma((chips,)),
+            dma((chips, 4)),
+            dma((chips, 4)),
+            dma((chips, 4)),
             dma((3,)),
             dma((3,)),
         ],

time: 93.5 us -> 79.8 us (0.85)
  Pallas kernels: 91.6 us -> 77.6 us
    pallas_call x1, Pallas kernels: 90.1 us -> 76.1 us  [fused(): pl.pallas_call(functools.partial(fused_kernel, (local_count, planes, chip...]
where the time goes in v4:
time: 79.8 us; the launch traced here: 79.3 us
  Pallas kernels  77.6 us (97%)
  local copies, waits for them, and re-layouts  1.04 us (1%)
    pallas_call x1, Pallas kernels, fused(): pl.pallas_call(functools.partial(fused_kernel, (local_count, planes, chip...  76.1 us

profile of v4, /device:TPU:17, one launch (start us, length us, event | category | flops | bytes accessed | tf_op | source)
XLA Modules:
  0.0 79.3 jit_solution(1946392549482231591)
XLA Ops:
  0.6 0.0 copy-start
  0.6 76.1 %shard_map.104.x_ref = bf16[4,256,256]{2,1,0:T(8,128)(2,1)} custom-call(bf16[512,2048]{1,0:T(8,128)(2,1)} %bitcast.3, bf16[4,2048,512]{2,1,0:T(8,128)(2,1)} %constant.10.clone.table_ref, bf16[512,1024]{1,0:T(8,128)(2,1)} %constant.11.clone.cos_ref, bf16[512,1024]{1,0:T(8,128)(2,1)} %constant.12.clone.sin_ref, bf16[256,256]{1,0:T(8,128)(2,1)} %constant.13.clone.update_ref, ...), custom_call_target="tpu_custom_call" | custom-call | flops 14000000000 | bytes 20971520 | tf_op jit(solution)/shard_map/pallas_call | solution.py:577
  76.7 0.0 copy-done
  76.7 0.0 copy-start.1
  76.7 1.0 %copy-done.1 = bf16[4,256,256]{2,1,0:T(8,128)(2,1)S(1)} copy-done((bf16[4,256,256]{2,1,0:T(8,128)(2,1)S(1)}, bf16[4,256,256]{2,1,0:T(8,128)(2,1)}, u32[]{:S(2)}) %copy-start.1) | copy-done | bytes 524312
  77.8 1.6 %shard_map.105 = (f32[256,512]{1,0:T(8,128)}, f32[256,512]{1,0:T(8,128)}) custom-call(bf16[4,256,256]{2,1,0:T(8,128)(2,1)S(1)} %copy-done.1, bf16[4,2,512,512]{3,2,1,0:T(8,128)(2,1)S(1)} %copy-done), custom_call_target="tpu_custom_call" | custom-call | tf_op jit(solution)/shard_map/pallas_call | solution.py:646
Async XLA Ops:
  0.6 76.1 %copy-start = (bf16[4,2,512,512]{3,2,1,0:T(8,128)(2,1)S(1)}, bf16[4,2,512,512]{3,2,1,0:T(8,128)(2,1)}, u32[]{:S(2)}) copy-start(bf16[4,2,512,512]{3,2,1,0:T(8,128)(2,1)} %constant.14.clone.place_ref) | copy-start | bytes 12582916
  76.7 1.0 %copy-start.1 = (bf16[4,256,256]{2,1,0:T(8,128)(2,1)S(1)}, bf16[4,256,256]{2,1,0:T(8,128)(2,1)}, u32[]{:S(2)}) copy-start(bf16[4,256,256]{2,1,0:T(8,128)(2,1)} %shard_map.104.x_ref) | copy-start | bytes 1572868
